TPU v7x, 32 devices: a whole 2x2x4 slice. The times are simulated.
32 devices in a mesh: seq: 4 (over y, x), dp: 8 (over z, core).
Axes of the slice: x: 2, y: 2, z: 4, core: 2. Of those that a mesh axis runs over, the one named last changes fastest.
Arguments:
- codes: int32 [16, 3072], P('dp', 'seq'), may hold values from 0 to 511
- actions: int32 [16, 3072], P('dp', 'seq'), may hold values from 0 to 17
- next_codes: int32 [16, 3072], P('dp', 'seq'), may hold values from 0 to 511
- lengths: int32 [16, 8], P('dp'), may hold values from 0 to 3072, as said below
- rewards: float32 [16, 3072], P('dp', 'seq'), may hold values from -6 to 6
- continues: float32 [16, 3072], P('dp', 'seq'), may hold values from 0 to 1
- target_values: float32 [16, 3072], P('dp', 'seq'), may hold values from -6 to 6
- table: float32 [530, 256], replicated, may hold values from -6 to 6
- table_m: float32 [530, 256], replicated, may hold values from -1.1444092e-05 to 1.1444092e-05
- table_v: float32 [530, 256], replicated, may hold values from 5.41632e-14 to 2.166528e-13
- attn_in: float32 [2, 256, 768], replicated, may hold values from -0.375 to 0.375
- attn_in_m: float32 [2, 256, 768], replicated, may hold values from -6.1035156e-05 to 6.1035156e-05
- attn_in_v: float32 [2, 256, 768], replicated, may hold values from 1.35408e-12 to 5.41632e-12
- attn_out: float32 [2, 256, 256], replicated, may hold values from -1 to 1
- attn_out_m: float32 [2, 256, 256], replicated, may hold values from -6.1035156e-05 to 6.1035156e-05
- attn_out_v: float32 [2, 256, 256], replicated, may hold values from 1.35408e-12 to 5.41632e-12
- ffn_in: float32 [2, 256, 1024], replicated, may hold values from -0.375 to 0.375
- ffn_in_m: float32 [2, 256, 1024], replicated, may hold values from -6.1035156e-05 to 6.1035156e-05
- ffn_in_v: float32 [2, 256, 1024], replicated, may hold values from 1.35408e-12 to 5.41632e-12
- ffn_out: float32 [2, 1024, 256], replicated, may hold values from -0.1875 to 0.1875
- ffn_out_m: float32 [2, 1024, 256], replicated, may hold values from -6.1035156e-05 to 6.1035156e-05
- ffn_out_v: float32 [2, 1024, 256], replicated, may hold values from 1.35408e-12 to 5.41632e-12
- gains: float32 [5, 256], replicated, may hold values from 0.5 to 1.5
- gains_m: float32 [5, 256], replicated, may hold values from -6.1035156e-05 to 6.1035156e-05
- gains_v: float32 [5, 256], replicated, may hold values from 1.35408e-12 to 5.41632e-12
- readout: float32 [256, 533], replicated, may hold values from -0.375 to 0.375
- readout_m: float32 [256, 533], replicated, may hold values from -6.1035156e-05 to 6.1035156e-05
- readout_v: float32 [256, 533], replicated, may hold values from 1.35408e-12 to 5.41632e-12
Outputs:
- table_new: float32 [530, 256], replicated
- table_m_new: float32 [530, 256], replicated
- table_v_new: float32 [530, 256], replicated
- attn_in_new: float32 [2, 256, 768], replicated
- attn_in_m_new: float32 [2, 256, 768], replicated
- attn_in_v_new: float32 [2, 256, 768], replicated
- attn_out_new: float32 [2, 256, 256], replicated
- attn_out_m_new: float32 [2, 256, 256], replicated
- attn_out_v_new: float32 [2, 256, 256], replicated
- ffn_in_new: float32 [2, 256, 1024], replicated
- ffn_in_m_new: float32 [2, 256, 1024], replicated
- ffn_in_v_new: float32 [2, 256, 1024], replicated
- ffn_out_new: float32 [2, 1024, 256], replicated
- ffn_out_m_new: float32 [2, 1024, 256], replicated
- ffn_out_v_new: float32 [2, 1024, 256], replicated
- gains_new: float32 [5, 256], replicated
- gains_m_new: float32 [5, 256], replicated
- gains_v_new: float32 [5, 256], replicated
- readout_new: float32 [256, 533], replicated
- readout_m_new: float32 [256, 533], replicated
- readout_v_new: float32 [256, 533], replicated
- loss_sum: float32 [], replicated
- step_count: float32 [], replicated
- grad_norm: float32 [], replicated
Inputs may be any that keep to these rules, and one draw needn't show every extreme that they name: Each sequence's lengths sum to 3072; lengths may be 0; in each block of 2 sequences one sequence is a single episode.
All inputs are finite; a program needn't handle non-finite values.
Results may differ from a plain program's by a relative error of at most 0.0066.
Values may be sent and summed in bfloat16 or wider, within the bound.
A program may use at most 256 MiB of HBM per device.

v0:
```python
import functools
import math

import jax
import jax.numpy as jnp
import numpy as np
from jax import lax
from jax.experimental import pallas as pl
from jax.experimental.pallas import tpu as pltpu
from jax.sharding import PartitionSpec as P

HEADS = 8
VOCAB = 512
SEG = 48
STEP = 5

EPS_NORM = 1e-06
BETA_ONE = 0.9
BETA_TWO = 0.999
RATES = (0.25, 0.02, 0.08, 0.02, 0.02, 0.25, 0.02)
DECAY = 0.01
ADAM_EPS = 1e-08
CLIP_NORM = 0.05
GAMMA = 0.985
LAMBDA_RET = 0.95
ENTROPY_COEF = 0.05

BF = jnp.bfloat16
F32 = jnp.float32
ROWS = 256
QRY = 2 * SEG
KEY = 3 * SEG
OUTS = 544
NEG = -1e30
MESH = pl.DeviceIdType.MESH
PER_ROW = 256 / 92e3
TRANSFERS = {
    "core": ("core", PER_ROW / 5.4, 1.1),
    "seq": ("seq", PER_ROW, 3.3),
    "deep": ("deep", PER_ROW / 2, 3.5),
    "tile": ("tile", 0.0, 3.6),
}
PATH = ("core", "seq", "deep", "back_deep", "back_seq", "back_core")
STAGE_TIME = 0.35


def dot_nn(left, right):
    return jnp.dot(left, right, preferred_element_type=F32)


def dot_tn(left, right):
    return lax.dot_general(left, right, (((0,), (0,)), ((), ())), preferred_element_type=F32)


def dot_nt(left, right):
    return lax.dot_general(left, right, (((1,), (1,)), ((), ())), preferred_element_type=F32)


def iota(shape, dim):
    return lax.broadcasted_iota(jnp.int32, shape, dim)


def rms_apply(x, gain):
    inv = lax.rsqrt(jnp.mean(x * x, axis=-1, keepdims=True) + EPS_NORM)
    return (x * inv * gain).astype(BF)


def rms_pull(grad, x, gain):
    inv = lax.rsqrt(jnp.mean(x * x, axis=-1, keepdims=True) + EPS_NORM)
    unit = x * inv
    weighted = grad * gain
    grad_x = inv * (weighted - unit * jnp.mean(weighted * unit, axis=-1, keepdims=True))
    rows, dims = x.shape
    return grad_x, jnp.sum((grad * unit).reshape(rows // 8, 8, dims), axis=0)


def grad_row_count(layers):
    rows = VOCAB + layers * 12 * 256 + OUTS + (OUTS - VOCAB) + 16
    return -(-rows // 256) * 256


def buckets_of(layers):
    cuts = [0, VOCAB + 4 * 256]
    for layer in range(layers):
        cuts.append(cuts[-1] + 5 * 256)
        cuts.append(cuts[-1] + (3 if layer == layers - 1 else 7) * 256)
    cuts.append(grad_row_count(layers))
    return list(zip(cuts[:-1], cuts[1:]))


def owners_of(bucket, seq_size, deep):
    quarter = (bucket[1] - bucket[0]) // seq_size
    return max(k for k in range(1, deep + 1) if quarter % (16 * k) == 0)


class Exchange:
    def __init__(self, seq_size, dp_size, buckets, grads, out, core_in, seq_in, seq_out, deep_in,
                 squares, tile_out, tile_in, send_sem, recv_sem, out_sem):
        self.deep = dp_size // 2
        self.seq_size = seq_size
        self.buckets = buckets
        self.grads, self.out = grads, out
        self.core_in, self.seq_in, self.seq_out, self.deep_in = core_in, seq_in, seq_out, deep_in
        self.squares = squares
        self.tile_out, self.tile_in = tile_out, tile_in
        self.send_sem, self.recv_sem, self.out_sem = send_sem, recv_sem, out_sem
        self.slots = exchange_slots(dp_size)
        me = lax.axis_index("seq")
        at_dp = lax.axis_index("dp")
        self.me, self.core, self.at_deep = me, lax.rem(at_dp, 2), lax.div(at_dp, 2)
        self.sibling = {"dp": self.at_deep * 2 + 1 - self.core}
        self.stage, self.due, self.free, self.now, self.summed = {}, {}, {}, 0.0, 0

    def deep_peer(self, k):
        return {"dp": lax.rem(self.at_deep + k, self.deep) * 2 + self.core}

    def peers(self):
        found = [self.sibling]
        found += [{"seq": lax.rem(self.me + k, self.seq_size)} for k in range(1, self.seq_size)]
        return found + [self.deep_peer(k) for k in range(1, self.deep)]

    def greet(self):
        for peer in self.peers():
            pl.semaphore_signal(
                pltpu.get_barrier_semaphore(), inc=1, device_id=peer, device_id_type=MESH
            )

    def greeted(self):
        pl.semaphore_wait(pltpu.get_barrier_semaphore(), len(self.peers()))

    def copy(self, src, dst, n, slot, peer):
        return pltpu.make_async_remote_copy(
            src_ref=src,
            dst_ref=dst,
            send_sem=self.send_sem.at[n, slot],
            recv_sem=self.recv_sem.at[n, slot],
            device_id=peer,
            device_id_type=MESH,
        )

    def only(self, n, index, act):
        owners = owners_of(self.buckets[n], self.seq_size, self.deep)
        if owners == self.deep:
            act()
        else:
            pl.when(index < owners)(act)

    def parts(self, n):
        r0, r1 = self.buckets[n]
        quarter = (r1 - r0) // self.seq_size
        return r0, r1 - r0, quarter, quarter // owners_of(self.buckets[n], self.seq_size, self.deep)

    def place(self, n, index):
        return lax.rem(index, owners_of(self.buckets[n], self.seq_size, self.deep))

    def deep_rows(self, n):
        at = sum(self.parts(k)[3] for k in range(n))
        return pl.ds(at, self.parts(n)[3])

    def quarter_rows(self, n, index):
        r0, _, quarter, _ = self.parts(n)
        return pl.ds(pl.multiple_of(r0 + index * quarter, 16), quarter)

    def packed_rows(self, n):
        r0, _, quarter, _ = self.parts(n)
        return pl.ds(r0 // self.seq_size, quarter)

    def share_rows(self, n, index):
        r0, _, _, share = self.parts(n)
        return pl.ds(pl.multiple_of(r0 // self.seq_size + index * share, 16), share)

    def own_rows(self, n):
        r0, _, quarter, share = self.parts(n)
        at = r0 + self.me * quarter + self.place(n, self.at_deep) * share
        return pl.ds(pl.multiple_of(at, 16), share)

    def blocks(self, n, index, work):
        r0, _, quarter, _ = self.parts(n)
        size = quarter // 2 if quarter > 256 else quarter
        for at in range(0, quarter, size):
            wide = pl.ds(pl.multiple_of(r0 + index * quarter + at, 16), size)
            work(wide, pl.ds(r0 // self.seq_size + at, size))

    def core_copies(self, n):
        r0, rows, _, _ = self.parts(n)
        part = pl.ds(r0, rows)
        return [self.copy(self.grads.at[1 - self.core, part], self.core_in.at[part], n, 0, self.sibling)]

    def seq_copies(self, n):
        packed = self.packed_rows(n)
        found = []
        for k in range(1, self.seq_size):
            peer = lax.rem(self.me + k, self.seq_size)
            source = self.core_in.at[self.quarter_rows(n, peer)]
            found.append(self.copy(source, self.seq_in.at[k - 1, packed], n, k, {"seq": peer}))
        return found

    def deep_copy(self, n, k):
        target = self.place(n, lax.rem(self.at_deep + k, self.deep))
        dest = self.deep_in.at[k - 1, self.deep_rows(n)]
        return self.copy(self.seq_out.at[self.share_rows(n, target)], dest, n, 3 + k, self.deep_peer(k))

    def back_copy(self, n, rows, slot, peer):
        there = self.grads.at[self.core, rows]
        return self.copy(there, there, n, self.slots // 2 + slot, peer)

    def back_seq(self, n):
        rows = self.quarter_rows(n, self.me)
        return [
            self.back_copy(n, rows, k, {"seq": lax.rem(self.me + k, self.seq_size)})
            for k in range(1, self.seq_size)
        ]

    def back_core(self, n):
        r0, rows, _, _ = self.parts(n)
        return [self.back_copy(n, pl.ds(r0, rows), 0, self.sibling)]

    def out_copies(self, n):
        r0, rows, _, _ = self.parts(n)
        part = pl.ds(r0, rows)
        return [
            pltpu.make_async_copy(self.grads.at[side, part], self.out.at[side, part], self.out_sem.at[n, side])
            for side in range(2)
        ]

    def start(self, copies):
        for copy in copies:
            copy.start()

    def wait(self, copies):
        for copy in copies:
            copy.wait()

    def own_sum(self, wide, packed):
        both = self.grads[self.core, wide, :].astype(F32) + self.core_in[wide, :].astype(F32)
        for k in range(self.seq_size - 1):
            both = both + self.seq_in[k, packed, :].astype(F32)
        return both

    def after_core(self, n):
        def work(wide, packed):
            both = self.grads[self.core, wide, :].astype(F32) + self.core_in[wide, :].astype(F32)
            self.core_in[wide, :] = both.astype(BF)

        for k in range(1, self.seq_size):
            self.blocks(n, lax.rem(self.me + k, self.seq_size), work)

    def after_seq(self, n):
        def work(wide, packed):
            self.seq_out[packed, :] = self.own_sum(wide, packed).astype(BF)

        self.blocks(n, self.me, work)

    def after_deep(self, n):
        share = self.parts(n)[3]

        def act():
            rows = self.own_rows(n)
            both = self.own_sum(rows, self.share_rows(n, self.place(n, self.at_deep)))
            part = self.deep_rows(n)
            for k in range(self.deep - 1):
                both = both + self.deep_in[k, part, :].astype(F32)
            self.grads[self.core, rows, :] = both.astype(BF)
            self.squares[...] += jnp.sum((both * both).reshape(share // 8, 8, both.shape[1]), axis=0)

        self.only(n, self.at_deep, act)

    def begin_deep(self, n):
        for k in range(1, self.deep):
            target = lax.rem(self.at_deep + k, self.deep)
            self.only(n, target, self.deep_copy(n, k).start)

    def end_deep(self, n):
        for k in range(1, self.deep):
            target = lax.rem(self.at_deep + k, self.deep)
            self.only(n, target, self.deep_copy(n, k).wait_send)

        def act():
            for k in range(1, self.deep):
                self.deep_copy(n, k).wait_recv()

        self.only(n, self.at_deep, act)

    def begin_back_deep(self, n):
        rows = self.own_rows(n)

        def act():
            for k in range(1, self.deep):
                self.back_copy(n, rows, 3 + k, self.deep_peer(k)).start()

        self.only(n, self.at_deep, act)

    def end_back_deep(self, n):
        rows = self.own_rows(n)

        def act():
            for k in range(1, self.deep):
                self.back_copy(n, rows, 3 + k, self.deep_peer(k)).wait_send()

        self.only(n, self.at_deep, act)
        for k in range(1, self.deep):
            origin = lax.rem(self.at_deep + self.deep - k, self.deep)
            self.only(n, origin, self.back_copy(n, rows, 3 + k, self.deep_peer(k)).wait_recv)

    def begin_transfer(self, n, name):
        if name == "deep":
            self.begin_deep(n)
        elif name == "back_deep":
            self.begin_back_deep(n)
        else:
            self.start(getattr(self, name if "back" in name else name + "_copies")(n))

    def end_transfer(self, n, name):
        if name == "deep":
            self.end_deep(n)
        elif name == "back_deep":
            self.end_back_deep(n)
        else:
            self.wait(getattr(self, name if "back" in name else name + "_copies")(n))
        if name == "core":
            self.after_core(n)
        elif name == "seq":
            self.after_seq(n)
        elif name == "deep":
            self.after_deep(n)
        elif name == "back_core":
            self.start(self.out_copies(n))

    def plan_launch(self, n):
        if n < len(self.buckets):
            name, rows = PATH[self.stage[n]], self.buckets[n][1] - self.buckets[n][0]
        else:
            name, rows = "tile", 0
        link, share, latency = TRANSFERS[name.replace("back_", "")]
        self.free[link] = max(self.now, self.free.get(link, 0.0)) + rows * share
        self.due[n] = self.free[link] + latency

    def plan_begin(self, n):
        self.stage[n] = 0
        self.plan_launch(n)
        return (n, None, 0)

    def plan_advance(self, n):
        step = self.stage[n]
        self.now = max(self.now, self.due.pop(n)) + STAGE_TIME
        self.stage[n] += 1
        last = (len(PATH) if n < len(self.buckets) else 3) - 1
        if step < last:
            self.plan_launch(n)
        todo = [(n, step, step + 1 if step < last else None)]
        if n < len(self.buckets):
            self.summed += PATH[step] == "deep"
        norm = len(self.buckets) + 1
        if self.summed == len(self.buckets) and norm not in self.stage:
            todo.append(self.plan_begin(norm))
        return todo

    def plan(self, spent):
        self.now += spent
        todo = []
        for n in sorted(self.due):
            if self.due[n] + 0.3 <= self.now:
                todo += self.plan_advance(n)
        return todo

    def run(self, todo):
        for n, ended, begun in todo:
            if n < len(self.buckets):
                if ended is not None:
                    self.end_transfer(n, PATH[ended])
                if begun is not None:
                    self.begin_transfer(n, PATH[begun])
            else:
                tile = n - len(self.buckets)
                if tile == 1 and ended is None:
                    self.tile_out[1, 0] = self.squares[...]
                if ended is not None:
                    self.tile_finish(tile, ended)
                if begun is not None:
                    self.tile_start(tile, begun)

    def begin(self, n):
        self.run([self.plan_begin(n)])

    def tick(self, spent):
        self.run(self.plan(spent))

    def drain(self):
        while self.due:
            self.run(self.plan_advance(min(self.due, key=lambda n: (self.due[n], n))))

    def tile_copies(self, tile, phase):
        if phase == 0:
            slots, peers = [0], [self.sibling]
        elif phase == 1:
            slots = list(range(1, self.seq_size))
            peers = [{"seq": lax.rem(self.me + k, self.seq_size)} for k in slots]
        else:
            slots = [3 + k for k in range(1, self.deep)]
            peers = [self.deep_peer(k) for k in range(1, self.deep)]
        n = len(self.buckets) + tile
        return [
            self.copy(self.tile_out.at[tile, phase], self.tile_in.at[tile, slot], n, slot, peer)
            for slot, peer in zip(slots, peers)
        ], slots

    def tile_start(self, tile, phase):
        self.start(self.tile_copies(tile, phase)[0])

    def tile_finish(self, tile, phase):
        copies, slots = self.tile_copies(tile, phase)
        self.wait(copies)
        both = self.tile_out[tile, phase]
        for slot in slots:
            both = both + self.tile_in[tile, slot]
        self.tile_out[tile, phase + 1] = both


def exchange_slots(dp_size):
    return 2 * (4 + dp_size // 2 - 1)


def step_kernel(
    layers,
    sizes,
    buckets,
    codes_ref,
    actions_ref,
    next_ref,
    lengths_ref,
    rewards_ref,
    continues_ref,
    values_ref,
    trig_ref,
    table_ref,
    attn_in_ref,
    attn_out_ref,
    ffn_in_ref,
    ffn_out_ref,
    gains_ref,
    readout_ref,
    out_ref,
    scal_ref,
    wq,
    wo,
    wu,
    wd,
    rt,
    tb,
    xs,
    hs,
    qs,
    kvs,
    probs,
    acts,
    gds,
    mixes,
    lows,
    tokf,
    toki,
    gouts,
    gx,
    gl,
    dmix,
    dqkv,
    carried,
    dgain,
    lossacc,
    lam,
    bsend,
    brecv,
    send_sem,
    recv_sem,
    load_sem,
    table_f,
    readout_f,
    grads_ref,
    *exchange_refs,
):
    batch, span = codes_ref.shape
    dims = gains_ref.shape[1]
    ff = ffn_in_ref.shape[2]
    tiles = span // SEG
    pairs = span // QRY
    total = batch * span
    chunks = total // ROWS
    per_seq = span // ROWS
    vocab_all = table_ref.shape[0]
    outs_all = readout_ref.shape[0]
    head_dim = dims // HEADS
    scale = head_dim ** (-0.5)
    exp_scale = scale * math.log2(math.e)
    groups = HEADS // 2
    base = lax.axis_index("seq") * span
    me = lax.axis_index("seq")
    seq_size = sizes[0]
    right = lax.rem(me + 1, seq_size)
    left = lax.rem(me + seq_size - 1, seq_size)

    ex = Exchange(*sizes, buckets, grads_ref, out_ref, *exchange_refs)
    ex.greet()
    ex.squares[...] = jnp.zeros_like(ex.squares)

    loads = [
        pltpu.make_async_copy(table_ref, table_f, load_sem.at[0]),
        pltpu.make_async_copy(readout_ref, readout_f, load_sem.at[1]),
    ]
    blocks = []
    for layer in range(layers):
        for j in range(3):
            blocks.append((attn_in_ref, wq, layer, slice(0, 256), slice(j * 256, j * 256 + 256)))
        blocks.append((attn_out_ref, wo, layer, slice(0, 256), slice(0, 256)))
        for j in range(ff // 256):
            blocks.append((ffn_in_ref, wu, layer, slice(0, 256), slice(j * 256, j * 256 + 256)))
        for j in range(ff // 256):
            blocks.append((ffn_out_ref, wd, layer, slice(j * 256, j * 256 + 256), slice(0, 256)))

    def place_of(k):
        at = (k + (2 * layers - 2) * chunks) % (2 * layers * chunks)
        return 1 + at // chunks, slice(256 * (at % chunks), 256 * (at % chunks) + 256)

    for k, (source, _, layer, rows, cols) in enumerate(blocks):
        plane, there = place_of(k)
        loads.append(
            pltpu.make_async_copy(source.at[layer, rows, cols], xs.at[plane, there, :], load_sem.at[2 + k])
        )
    for load in loads:
        load.start()

    def convert(low, high):
        for k in range(low, high):
            _, dest, layer, rows, cols = blocks[k]
            plane, there = place_of(k)
            loads[2 + k].wait()
            dest[layer, rows, cols] = xs[plane, there, :].astype(BF)

    tb[...] = jnp.zeros_like(tb)
    rt[...] = jnp.zeros_like(rt)

    ends = []
    for b in range(batch):
        run = jnp.int32(0)
        row = []
        for e in range(lengths_ref.shape[1]):
            run = run + lengths_ref[b, e]
            row.append(run)
        ends.append(row)
    episodes = len(ends[0])

    lane = iota((8, span), 1)
    lam[...] = jnp.zeros_like(lam)
    lam[0, 0:batch, :] = rewards_ref[...]
    lam[1, 0:batch, :] = continues_ref[...]
    lam[2, 0:batch, :] = values_ref[...]
    last = lax.rem(lane, SEG) == SEG - 1
    decay = GAMMA * lam[1]
    value_next = pltpu.roll(lam[2], span - 1, 1)
    add = jnp.where(last, lam[2], lam[0] + decay * ((1.0 - LAMBDA_RET) * value_next))
    mul = jnp.where(last, 0.0, decay * LAMBDA_RET)
    step = 1
    while step < SEG:
        add = add + mul * pltpu.roll(add, span - step, 1)
        mul = mul * pltpu.roll(mul, span - step, 1)
        step *= 2
    lam[3] = add
    valid_rows = []
    for b in range(batch):
        after = iota((1, span), 1) + (base + 1)
        final = after == ends[b][0]
        for e in range(1, episodes):
            final = final | (after == ends[b][e])
        valid_rows.append(jnp.where(final, 0.0, 1.0))
    for c in range(chunks):
        b = c // per_seq
        lanes = slice((c % per_seq) * ROWS, (c % per_seq) * ROWS + ROWS)
        for row in range(4):
            tokf[c, row : row + 1, :] = lam[row, b : b + 1, lanes]
        tokf[c, 4:5, :] = valid_rows[b][:, lanes]
        toki[c, 0:1, :] = codes_ref[b : b + 1, lanes]
        toki[c, 1:2, :] = actions_ref[b : b + 1, lanes]
        toki[c, 2:3, :] = next_ref[b : b + 1, lanes]

    half = dims // 2
    in_sin, in_cos = trig_ref[0:SEG, 2, :], trig_ref[0:SEG, 3, :]
    end_sin, end_cos = [], []
    for b in range(batch):
        for e in range(episodes):
            far, near = lax.div(ends[b][e], SEG), lax.rem(ends[b][e], SEG)
            far_sin, far_cos = trig_ref[far, 0:1, :], trig_ref[far, 1:2, :]
            near_sin, near_cos = trig_ref[near, 2:3, :], trig_ref[near, 3:4, :]
            end_sin.append(far_sin * near_cos + far_cos * near_sin)
            end_cos.append(far_cos * near_cos - far_sin * near_sin)

    def marks(tile, carry):
        at = me * tiles + tile
        tile_sin, tile_cos = trig_ref[at, 0:1, :], trig_ref[at, 1:2, :]
        here_sin = in_sin * tile_cos + in_cos * tile_sin
        here_cos = in_cos * tile_cos - in_sin * tile_sin
        place = iota((SEG, half), 0) + (base + tile * SEG)
        for b in range(batch):
            start_sin = jnp.zeros((SEG, half), F32)
            start_cos = jnp.ones((SEG, half), F32)
            for e in range(episodes):
                passed = place >= ends[b][e]
                row = b * episodes + e
                start_sin = jnp.where(passed, end_sin[row], start_sin)
                start_cos = jnp.where(passed, end_cos[row], start_cos)
            rows = pl.ds(pl.multiple_of(b * span + tile * SEG, SEG), SEG)
            xs[0, rows, 0:half] = here_sin * start_cos - here_cos * start_sin
            xs[0, rows, half:dims] = here_cos * start_cos + here_sin * start_sin
        return carry

    lax.fori_loop(0, tiles, marks, 0)

    def lowest(pair, carry):
        within = lax.rem(iota((8, groups * QRY), 1), QRY)
        first = base + pair * QRY - SEG
        place = within + (base + pair * QRY)
        for b in range(batch):
            low = jnp.where(within >= SEG, SEG, 0)
            for e in range(episodes):
                low = jnp.where(place >= ends[b][e], jnp.maximum(low, ends[b][e] - first), low)
            lows[b * pairs + pair] = jnp.maximum(low, -first)
        return carry

    lax.fori_loop(0, pairs, lowest, 0)

    def chunk_rows(c):
        return pl.ds(pl.multiple_of(c * ROWS, ROWS), ROWS)

    def kv_rows(c):
        return pl.ds(pl.multiple_of(lax.rem(c, per_seq) * ROWS + SEG, 16), ROWS)

    loads[0].wait()
    tb[0:vocab_all, :] = table_f[...].astype(BF)

    def onehot(c):
        code = toki[c, 0:1, :]
        act = toki[c, 1:2, :] + VOCAB
        ids = iota((OUTS, ROWS), 0)
        return jnp.where((ids == code) | (ids == act), 1.0, 0.0).astype(BF)

    def both_chunks(i):
        return (2 * i, 2 * i + 1)

    def embed(i, carry):
        for c in both_chunks(i):
            xs[0, chunk_rows(c), :] += dot_tn(onehot(c), tb[...])
        return carry

    lax.fori_loop(0, chunks // 2, embed, 0)

    lane_head = iota((1, dims), 1) // head_dim
    group_mask = [jnp.where(lane_head // 2 == g, 1.0, 0.0).astype(BF) for g in range(groups)]
    even_mask = jnp.where(lax.rem(lane_head, 2) == 0, 1.0, 0.0).astype(BF)
    odd_mask = jnp.where(lax.rem(lane_head, 2) == 1, 1.0, 0.0).astype(BF)
    even_f = lax.rem(lane_head, 2) == 0

    def by_group(rows):
        return jnp.concatenate([rows * group_mask[g] for g in range(groups)], axis=0)

    def both(keys):
        return jnp.concatenate([keys * even_mask, keys * odd_mask], axis=0)

    def gather_heads(wide):
        out = wide[0:QRY]
        for g in range(1, groups):
            out = jnp.where(lane_head // 2 == g, wide[g * QRY : g * QRY + QRY], out)
        return out

    def forward_copy(layer):
        return pltpu.make_async_remote_copy(
            src_ref=kvs.at[layer, :, pl.ds(span, SEG), :],
            dst_ref=kvs.at[layer, :, pl.ds(0, SEG), :],
            send_sem=send_sem.at[layer],
            recv_sem=recv_sem.at[layer],
            device_id={"seq": right},
            device_id_type=MESH,
        )

    def backward_copy(layer):
        return pltpu.make_async_remote_copy(
            src_ref=bsend.at[layer],
            dst_ref=brecv.at[layer],
            send_sem=send_sem.at[layers + layer],
            recv_sem=recv_sem.at[layers + layer],
            device_id={"seq": left},
            device_id_type=MESH,
        )

    def project(layer):
        gain = gains_ref[2 * layer : 2 * layer + 1, :]

        def body(i, carry):
            pieces = [(c, chunk_rows(c)) for c in both_chunks(i)]
            normed = [rms_apply(xs[2 * layer, rows, :], gain) for _, rows in pieces]
            wide = [dot_nn(h, wq[layer]).astype(BF) for h in normed]
            for (c, rows), h, qkv in zip(pieces, normed, wide):
                hs[2 * layer, rows, :] = h
                qs[layer, rows, :] = qkv[:, 0:dims]
                kvs[layer, c // per_seq, kv_rows(c), :] = qkv[:, dims:]
            return carry

        lax.fori_loop(0, chunks // 2, body, 0)

    def pair_rows(b, pair):
        return pl.ds(pl.multiple_of(b * span + pair * QRY, 16), QRY)

    def pair_window(pair):
        return pl.ds(pl.multiple_of(pair * QRY, 16), KEY)

    causal = iota((KEY, groups * QRY), 0) <= lax.rem(iota((KEY, groups * QRY), 1), QRY) + SEG
    key_place = iota((KEY, groups * QRY), 0)

    def attend(layer):
        copy = forward_copy(layer)

        def body(i, carry):
            items = [(b, pairs - 1 - 2 * i - j) for j in range(2) for b in range(batch)]
            pl.when(i == pairs // 2 - 1)(copy.wait)
            scores = []
            for b, pair in items:
                keys = kvs[layer, b, pair_window(pair), 0:dims]
                scores.append(dot_nt(both(keys), by_group(qs[layer, pair_rows(b, pair), :])))
            weights = []
            for (b, pair), score in zip(items, scores):
                seen = causal & (key_place >= lows[b * pairs + pair, 0:1, :])
                sides = []
                for side in range(2):
                    s = jnp.where(seen, score[side * KEY : side * KEY + KEY], NEG)
                    top = jnp.max(s, axis=0, keepdims=True)
                    e = jnp.exp2((s - top) * exp_scale)
                    sides.append((e * (1.0 / jnp.sum(e, axis=0, keepdims=True))).astype(BF))
                p = jnp.concatenate(sides, axis=0)
                probs[layer, b * pairs + pair] = p
                weights.append(p)
            for (b, pair), p in zip(items, weights):
                values = kvs[layer, b, pair_window(pair), dims:]
                wide = dot_tn(p, both(values))
                mixes[layer, pair_rows(b, pair), :] = gather_heads(wide).astype(BF)
            return carry

        copy.start()
        lax.fori_loop(0, pairs // 2, body, 0)

    def feed(layer):
        gain = gains_ref[2 * layer + 1 : 2 * layer + 2, :]
        c0, c1 = math.sqrt(2.0 / math.pi), 0.044715

        def body(i, carry):
            pieces = [chunk_rows(c) for c in both_chunks(i)]
            mids = [xs[2 * layer, rows, :] + dot_nn(mixes[layer, rows, :], wo[layer]) for rows in pieces]
            normed = [rms_apply(x, gain) for x in mids]
            for rows, x, h in zip(pieces, mids, normed):
                xs[2 * layer + 1, rows, :] = x
                hs[2 * layer + 1, rows, :] = h
            hidden = [[], []]
            for j in range(ff // 256):
                cols = slice(j * 256, j * 256 + 256)
                for rows, h, parts in zip(pieces, normed, hidden):
                    up = dot_nn(h, wu[layer, :, cols])
                    square = up * up
                    half_t = 0.5 + 0.5 * jnp.tanh(up * (c0 + (c0 * c1) * square))
                    act = up * half_t
                    slope = half_t + (1.0 - half_t) * act * (2.0 * c0 + (6.0 * c0 * c1) * square)
                    parts.append(act.astype(BF))
                    gds[layer, rows, cols] = slope.astype(BF)
            for rows, x, parts in zip(pieces, mids, hidden):
                act = jnp.concatenate(parts, axis=1)
                acts[layer, rows, :] = act
                xs[2 * layer + 2, rows, :] = x + dot_nn(act, wd[layer])
            return carry

        lax.fori_loop(0, chunks // 2, body, 0)

    per_layer = 4 + 2 * (ff // 256)
    for layer in range(layers):
        if layer == 0:
            convert(0, 3)
        project(layer)
        if layer == 0:
            ex.greeted()
        attend(layer)
        if layer == 0:
            convert(3, layers * per_layer)
        feed(layer)
    loads[1].wait()
    rt[0:outs_all, :] = readout_f[...].astype(BF)

    lossacc[...] = jnp.zeros_like(lossacc)
    dgain[...] = jnp.zeros_like(dgain)
    top_gain = gains_ref[2 * layers : 2 * layers + 1, :]

    def put(at, block):
        for side in range(2):
            cols = slice(side * 128, side * 128 + 128)
            grads_ref[side, at : at + block.shape[0], :] = block[:, cols].astype(BF)

    def loss_grad(c, outs):
        reward, cont = tokf[c, 0:1, :], tokf[c, 1:2, :]
        target, ret, valid = tokf[c, 2:3, :], tokf[c, 3:4, :], tokf[c, 4:5, :]
        action, code = toki[c, 1:2, :], toki[c, 2:3, :]
        logits = outs[0:VOCAB]
        top = jnp.max(logits, axis=0, keepdims=True)
        e = jnp.exp(logits - top)
        esum = jnp.sum(e, axis=0, keepdims=True)
        chosen = iota((VOCAB, ROWS), 0) == code
        picked = jnp.sum(jnp.where(chosen, logits, 0.0), axis=0, keepdims=True)
        loss = jnp.log(esum) + top - picked
        grad_logits = (e * (valid / esum) - jnp.where(chosen, valid, 0.0)).astype(BF)
        small = outs[VOCAB:OUTS]
        place = iota((OUTS - VOCAB, ROWS), 0)
        reward_err = small[0:1] - reward
        end_logit = small[1:2]
        value_err = small[2:3] - ret
        minus = jnp.exp(-jnp.abs(end_logit))
        soft = jnp.maximum(end_logit, 0.0) + jnp.log(1.0 + minus)
        sigmoid = jnp.where(end_logit >= 0.0, 1.0, minus) / (1.0 + minus)
        loss = loss + 0.5 * reward_err * reward_err + soft - cont * end_logit
        loss = loss + 0.5 * value_err * value_err
        actor = (place >= 3) & (place < outs_all - VOCAB)
        act_top = jnp.max(jnp.where(actor, small, NEG), axis=0, keepdims=True)
        act_e = jnp.where(actor, jnp.exp(jnp.where(actor, small - act_top, 0.0)), 0.0)
        act_sum = jnp.sum(act_e, axis=0, keepdims=True)
        log_pi = jnp.where(actor, small - act_top - jnp.log(act_sum), 0.0)
        pi = act_e / act_sum
        neg_entropy = jnp.sum(pi * log_pi, axis=0, keepdims=True)
        taken = place == action + 3
        picked_pi = jnp.sum(jnp.where(taken, log_pi, 0.0), axis=0, keepdims=True)
        gap = ret - target
        loss = loss - gap * picked_pi + ENTROPY_COEF * neg_entropy
        grad = gap * (pi - jnp.where(taken, 1.0, 0.0))
        grad = grad + ENTROPY_COEF * pi * (log_pi - neg_entropy)
        grad = jnp.where(actor, grad, 0.0)
        grad = jnp.where(place == 0, reward_err, grad)
        grad = jnp.where(place == 1, sigmoid - cont, grad)
        grad = jnp.where(place == 2, value_err, grad)
        lossacc[0:1, :] += loss * valid
        lossacc[1:2, :] += valid
        return jnp.concatenate([grad_logits, (grad * valid).astype(BF)], axis=0)

    def losses(i, carry):
        pieces = [(c, chunk_rows(c)) for c in both_chunks(i)]
        hidden = [xs[2 * layers, rows, :] for _, rows in pieces]
        normed = [rms_apply(x, top_gain) for x in hidden]
        outs = [dot_nt(rt[...], h) for h in normed]
        found = [loss_grad(c, out) for (c, _), out in zip(pieces, outs)]
        pulled = [dot_tn(grad, rt[...]) for grad in found]
        for (c, rows), x, h, grad, dh in zip(pieces, hidden, normed, found, pulled):
            hs[2 * layers, rows, :] = h
            gouts[:, rows] = grad
            grad_x, part = rms_pull(dh, x, top_gain)
            gx[rows, :] = grad_x
            gl[rows, :] = grad_x.astype(BF)
            dgain[2 * layers] += part
        return carry

    lax.fori_loop(0, chunks // 2, losses, 0)
    tail_at = VOCAB + layers * 12 * 256 + OUTS
    put(0, dot_nn(gouts[0:VOCAB, :], hs[2 * layers]))
    put(tail_at, dot_nn(gouts[VOCAB:OUTS, :], hs[2 * layers]))
    loss_total = jnp.sum(lossacc[0:1, :])
    count_total = jnp.sum(lossacc[1:2, :])
    place = iota(scal_ref.shape, 0)
    ex.tile_out[0, 0] = jnp.where(place == 0, loss_total, jnp.where(place == 1, count_total, 0.0))
    ex.begin(len(buckets))

    def spread(count, spent, body):
        plans = [ex.plan(spent / count) for _ in range(count)]

        def run(i, carry):
            body(i)
            for k, todo in enumerate(plans):
                if todo:
                    pl.when(i == k)(functools.partial(ex.run, todo))
            return carry

        lax.fori_loop(0, count, run, 0)

    def feed_back(layer):
        gain = gains_ref[2 * layer + 1 : 2 * layer + 2, :]

        def body(i):
            pieces = [chunk_rows(c) for c in both_chunks(i)]
            hidden = [[], []]
            for j in range(ff // 256):
                cols = slice(j * 256, j * 256 + 256)
                for rows, parts in zip(pieces, hidden):
                    da = dot_nt(gl[rows, :], wd[layer, cols, :])
                    parts.append((da * gds[layer, rows, cols].astype(F32)).astype(BF))
            hidden = [jnp.concatenate(parts, axis=1) for parts in hidden]
            pulled = [dot_nt(du, wu[layer]) for du in hidden]
            for rows, du, dh in zip(pieces, hidden, pulled):
                gds[layer, rows, :] = du
                grad_x, part = rms_pull(dh, xs[2 * layer + 1, rows, :], gain)
                dgain[2 * layer + 1] += part
                grad = gx[rows, :] + grad_x
                gx[rows, :] = grad
                low = grad.astype(BF)
                gl[rows, :] = low
                dmix[rows, :] = dot_nt(low, wo[layer]).astype(BF)

        spread(chunks // 2, 3.3, body)

    def attend_back(layer):
        def steps(i):
            items = [(b, 2 * i + j) for j in range(2) for b in range(batch)]
            keys, values, queries, douts = [], [], [], []
            for b, pair in items:
                window, rows = pair_window(pair), pair_rows(b, pair)
                keys.append(both(kvs[layer, b, window, 0:dims]))
                values.append(both(kvs[layer, b, window, dims:]))
                queries.append(by_group(qs[layer, rows, :]))
                douts.append(by_group(dmix[rows, :]))
            weights = [probs[layer, b * pairs + pair] for b, pair in items]
            pulled = [dot_nt(value, dout) for value, dout in zip(values, douts)]
            slopes = []
            for p, dp in zip(weights, pulled):
                sides = []
                for side in range(2):
                    part = slice(side * KEY, side * KEY + KEY)
                    pf = p[part].astype(F32)
                    d = dp[part]
                    sides.append((pf * (d - jnp.sum(d * pf, axis=0, keepdims=True))).astype(BF))
                slopes.append(jnp.concatenate(sides, axis=0))
            for (b, pair), ds, key in zip(items, slopes, keys):
                dqkv[pair_rows(b, pair), 0:dims] = (gather_heads(dot_tn(ds, key)) * scale).astype(BF)
            wide = []
            for ds, query, p, dout in zip(slopes, queries, weights, douts):
                dk = dot_nn(ds, query) * scale
                dv = dot_nn(p, dout)
                dk = jnp.where(even_f, dk[0:KEY], dk[KEY:])
                wide.append(jnp.concatenate([dk, jnp.where(even_f, dv[0:KEY], dv[KEY:])], axis=1))
            return items, wide

        def keep(items, wide):
            before = [carried[b] + wide[b][0:SEG] for b in range(batch)]
            for at, (b, pair) in enumerate(items):
                rows = pl.multiple_of(b * span + pair * QRY, 16)
                dqkv[pl.ds(rows, SEG), dims:] = wide[at][SEG:QRY].astype(BF)
                if at + batch < len(items):
                    ending = wide[at][QRY:] + wide[at + batch][0:SEG]
                    dqkv[pl.ds(pl.multiple_of(rows + SEG, 16), SEG), dims:] = ending.astype(BF)
                else:
                    carried[b] = wide[at][QRY:]
            return before

        copy = backward_copy(layer)

        def body(i):
            before = [rows.astype(BF) for rows in keep(*steps(i))]

            @pl.when(i == 0)
            def _():
                for b in range(batch):
                    bsend[layer, b] = before[b]
                copy.start()

            @pl.when(i > 0)
            def _():
                for b in range(batch):
                    rows = pl.ds(pl.multiple_of(b * span + i * 2 * QRY - SEG, 16), SEG)
                    dqkv[rows, dims:] = before[b]

        carried[...] = jnp.zeros_like(carried)
        spread(pairs // 2, 6.8, body)
        copy.wait()
        for b in range(batch):
            final = carried[b] + brecv[layer, b].astype(F32)
            dqkv[b * span + span - SEG : b * span + span, dims:] = final.astype(BF)

    def project_back(layer):
        gain = gains_ref[2 * layer : 2 * layer + 1, :]

        def body(i):
            pieces = [chunk_rows(c) for c in both_chunks(i)]
            pulled = [dot_nt(dqkv[rows, :], wq[layer]) for rows in pieces]
            for rows, dh in zip(pieces, pulled):
                grad_x, part = rms_pull(dh, xs[2 * layer, rows, :], gain)
                dgain[2 * layer] += part
                grad = gx[rows, :] + grad_x
                gx[rows, :] = grad
                gl[rows, :] = grad.astype(BF)

        spread(chunks // 2, 1.5, body)

    at = VOCAB
    bucket = 0
    for layer in reversed(range(layers)):
        for j in range(ff // 256):
            cols = slice(j * 256, j * 256 + 256)
            put(at, dot_tn(acts[layer, :, cols], gl[...]))
            at += 256
        ex.begin(bucket)
        ex.tick(1.2)
        feed_back(layer)
        for j in range(ff // 256):
            cols = slice(j * 256, j * 256 + 256)
            put(at, dot_tn(hs[2 * layer + 1], gds[layer, :, cols]))
            at += 256
            if j % 2:
                ex.tick(0.4)
        put(at, dot_tn(mixes[layer], gl[...]))
        at += 256
        ex.begin(bucket + 1)
        ex.tick(0.2)
        attend_back(layer)
        for j in range(3):
            cols = slice(j * 256, j * 256 + 256)
            put(at, dot_tn(hs[2 * layer], dqkv[:, cols]))
            at += 256
        bucket += 2
        if layer == 0:
            ex.begin(bucket)
        ex.tick(0.7)
        project_back(layer)

    def mark(c, carry):
        gouts[:, chunk_rows(c)] = onehot(c)
        return carry

    lax.fori_loop(0, chunks, mark, 0)
    put(at, dot_nn(gouts[...], gl[...]))
    ex.tick(1.6)
    at = tail_at + OUTS - VOCAB
    place = iota((16, dims), 0)
    gain_rows = jnp.zeros((16, dims), F32)
    for index in range(2 * layers + 1):
        gain_rows = jnp.where(place == index, jnp.sum(dgain[index], axis=0, keepdims=True), gain_rows)
    put(at, gain_rows)
    at += 16
    put(at, jnp.zeros((grads_ref.shape[1] - at, dims), F32))
    ex.begin(len(buckets) - 1)
    ex.drain()
    count = ex.tile_out[0, 3, 1:2, 0:1]
    norm = jnp.sqrt(jnp.sum(ex.tile_out[1, 3]) / (count * count))
    place = iota(scal_ref.shape, 0)
    scal = jnp.where(place == 2, norm, ex.tile_out[0, 3])
    scal_ref[...] = jnp.where(place == 3, jnp.minimum(1.0, CLIP_NORM / norm) / count, scal)
    for n in range(len(buckets)):
        ex.wait(ex.out_copies(n))


def gradients(codes, actions, next_codes, lengths, rewards, continues, values, weights, sizes):
    table, attn_in, attn_out, ffn_in, ffn_out, gains, readout = weights
    batch, span = codes.shape
    layers, dims, ff = ffn_in.shape
    total = batch * span
    tiles = span // SEG
    chunks = total // ROWS
    grad_rows = grad_row_count(layers)
    buckets = buckets_of(layers)
    seq_size, dp_size = sizes
    shares = [(b[1] - b[0]) // seq_size // owners_of(b, seq_size, dp_size // 2) for b in buckets]
    slots = exchange_slots(dp_size)
    hbm = pl.BlockSpec(memory_space=pltpu.HBM)
    steps = np.arange(lax.axis_size("seq") * tiles + 1, dtype=np.float64)[:, None]
    freq = np.exp(np.arange(dims // 2) * (-2.0 * math.log(10000.0) / dims))
    trig = np.zeros((steps.shape[0], 8, dims // 2), np.float32)
    trig[:, 0], trig[:, 1] = np.sin(steps * SEG * freq), np.cos(steps * SEG * freq)
    trig[:, 2], trig[:, 3] = np.sin(steps * freq), np.cos(steps * freq)
    trig = jnp.asarray(trig)
    vmem = pl.BlockSpec(memory_space=pltpu.VMEM)
    smem = pl.BlockSpec(memory_space=pltpu.SMEM)
    return pl.pallas_call(
        functools.partial(step_kernel, layers, sizes, buckets),
        out_shape=(
            jax.ShapeDtypeStruct((2, grad_rows, dims // 2), BF),
            jax.ShapeDtypeStruct((8, 128), F32),
        ),
        in_specs=[vmem] * 3 + [smem] + [vmem] * 4 + [hbm] * 5 + [vmem, hbm],
        out_specs=(hbm, vmem),
        scratch_shapes=[
            pltpu.VMEM((layers, dims, 3 * dims), BF),
            pltpu.VMEM((layers, dims, dims), BF),
            pltpu.VMEM((layers, dims, ff), BF),
            pltpu.VMEM((layers, ff, dims), BF),
            pltpu.VMEM((OUTS, dims), BF),
            pltpu.VMEM((OUTS, dims), BF),
            pltpu.VMEM((2 * layers + 1, total, dims), F32),
            pltpu.VMEM((2 * layers + 1, total, dims), BF),
            pltpu.VMEM((layers, total, dims), BF),
            pltpu.VMEM((layers, batch, SEG + span, 2 * dims), BF),
            pltpu.VMEM((layers, total // QRY, 2 * KEY, HEADS // 2 * QRY), BF),
            pltpu.VMEM((layers, total, ff), BF),
            pltpu.VMEM((layers, total, ff), BF),
            pltpu.VMEM((layers, total, dims), BF),
            pltpu.VMEM((total // QRY, 8, HEADS // 2 * QRY), jnp.int32),
            pltpu.VMEM((chunks, 8, ROWS), F32),
            pltpu.VMEM((chunks, 8, ROWS), jnp.int32),
            pltpu.VMEM((OUTS, total), BF),
            pltpu.VMEM((total, dims), F32),
            pltpu.VMEM((total, dims), BF),
            pltpu.VMEM((total, dims), BF),
            pltpu.VMEM((total, 3 * dims), BF),
            pltpu.VMEM((batch, SEG, 2 * dims), F32),
            pltpu.VMEM((2 * layers + 1, 8, dims), F32),
            pltpu.VMEM((8, ROWS), F32),
            pltpu.VMEM((4, 8, span), F32),
            pltpu.VMEM((layers, batch, SEG, 2 * dims), BF),
            pltpu.VMEM((layers, batch, SEG, 2 * dims), BF),
            pltpu.SemaphoreType.DMA((2 * layers,)),
            pltpu.SemaphoreType.DMA((2 * layers,)),
            pltpu.SemaphoreType.DMA((2 + 12 * layers,)),
            pltpu.VMEM(table.shape, F32),
            pltpu.VMEM(readout.shape, F32),
            pltpu.VMEM((2, grad_rows, dims // 2), BF),
            pltpu.VMEM((grad_rows, dims // 2), BF),
            pltpu.VMEM((seq_size - 1, grad_rows // seq_size, dims // 2), BF),
            pltpu.VMEM((grad_rows // seq_size, dims // 2), BF),
            pltpu.VMEM((dp_size // 2 - 1, sum(shares), dims // 2), BF),
            pltpu.VMEM((8, dims // 2), F32),
            pltpu.VMEM((2, 4, 8, 128), F32),
            pltpu.VMEM((2, slots // 2, 8, 128), F32),
            pltpu.SemaphoreType.DMA((len(buckets) + 2, slots)),
            pltpu.SemaphoreType.DMA((len(buckets) + 2, slots)),
            pltpu.SemaphoreType.DMA((len(buckets), 2)),
        ],
        compiler_params=pltpu.CompilerParams(
            collective_id=0, has_side_effects=True, vmem_limit_bytes=63 * 1024 * 1024
        ),
        name="train_step",
    )(
        codes,
        actions,
        next_codes,
        lengths,
        rewards,
        continues,
        values,
        trig,
        table,
        attn_in,
        attn_out,
        ffn_in,
        ffn_out,
        gains,
        readout,
    )


def adam_update(weight, first_mom, second_mom, clipped, rate):
    new_first = BETA_ONE * first_mom + (1.0 - BETA_ONE) * clipped
    new_second = BETA_TWO * second_mom + (1.0 - BETA_TWO) * clipped * clipped
    root = jnp.sqrt(new_second * (1.0 / (1.0 - BETA_TWO**STEP))) + ADAM_EPS
    ratio = new_first * (rate / (1.0 - BETA_ONE**STEP)) / root
    return (weight * (1.0 - rate * DECAY) - ratio, new_first, new_second)


AHEAD = 5


def update_kernel(layers, scal_ref, sums_ref, *refs):
    ins, outs, scalars, here = refs[0:21], refs[21:42], refs[42:45], refs[45:66]
    load_sem, store_sem, sum_sem, grads_ref = refs[66:]
    scale = scal_ref[3, 0]
    for k, ref in enumerate(scalars):
        ref[0, 0] = scal_ref[k, 0]
    pieces = [(slot, layer) for slot in (4, 3, 1, 2) for layer in range(layers)]
    pieces += [(0, None), (5, None), (6, None)]

    offset = VOCAB
    starts = {}
    for layer in reversed(range(layers)):
        starts[4, layer] = offset
        starts[3, layer] = offset + 4 * 256
        starts[2, layer] = offset + 8 * 256
        starts[1, layer] = offset + 9 * 256
        offset += 12 * 256
    table_at, tail_at = offset, offset + OUTS
    gains_at = tail_at + OUTS - VOCAB

    def view(ref, layer):
        return ref if layer is None else ref.at[layer]

    def moves(n, kind):
        slot, layer = pieces[n]
        for part in range(3):
            index = 3 * slot + part
            inside = view(here[index], layer)
            if kind == 0:
                yield pltpu.make_async_copy(view(ins[index], layer), inside, load_sem.at[n, part])
            else:
                yield pltpu.make_async_copy(inside, view(outs[index], layer), store_sem.at[n, part])

    def fetch(n):
        slot, layer = pieces[n]
        rows = {0: (table_at, OUTS), 6: (0, VOCAB), 5: (tail_at, sums_ref.shape[1] - tail_at)}
        if layer is not None:
            rows[slot] = (starts[slot, layer], here[3 * slot].shape[1] * here[3 * slot].shape[2] // 256)
        at, count = rows[slot]
        part = pl.ds(at, count)
        return pltpu.make_async_copy(sums_ref.at[:, part], grads_ref.at[:, part], sum_sem.at[n])

    def begin(n):
        for move in moves(n, 0):
            move.start()
        fetch(n).start()

    for n in range(AHEAD):
        begin(n)

    def renew(slot, layer, rows, cols, grad):
        refs = [view(here[3 * slot + part], layer) for part in range(3)]
        new = adam_update(*[ref[rows, cols] for ref in refs], grad.astype(F32) * scale, RATES[slot])
        for ref, value in zip(refs, new):
            ref[rows, cols] = value

    for n, (slot, layer) in enumerate(pieces):
        if n + AHEAD < len(pieces):
            begin(n + AHEAD)
        for move in moves(n, 0):
            move.wait()
        fetch(n).wait()
        if layer is not None:
            rows_all, cols_all = here[3 * slot].shape[1:]
            at = starts[slot, layer]
            for j in range(rows_all // 256):
                for i in range(cols_all // 256):
                    for side in range(2):
                        cols = slice(i * 256 + side * 128, i * 256 + side * 128 + 128)

                        def body(k, carry):
                            rows = pl.ds(pl.multiple_of(j * 256 + k * 64, 64), 64)
                            block = at + (j + i) * 256 + k * 64
                            grad = grads_ref[side, pl.ds(pl.multiple_of(block, 64), 64), :]
                            renew(slot, layer, rows, cols, grad)
                            return carry

                        lax.fori_loop(0, 4, body, 0)
        elif slot == 0:
            rows_all = here[0].shape[0]
            for side in range(2):
                cols = slice(side * 128, side * 128 + 128)

                def body(k, carry):
                    rows = pl.ds(pl.multiple_of(k * 64, 64), 64)
                    block = pl.ds(pl.multiple_of(table_at + k * 64, 64), 64)
                    renew(0, None, rows, cols, grads_ref[side, block, :])
                    return carry

                full = rows_all // 64
                lax.fori_loop(0, full, body, 0)
                if rows_all % 64:
                    last = slice(full * 64, rows_all)
                    block = grads_ref[side, table_at + full * 64 : tail_at, :]
                    renew(0, None, last, cols, block.astype(F32)[0 : rows_all % 64])
        elif slot == 6:
            outs_all = here[18].shape[0]
            for side in range(2):
                cols = slice(side * 128, side * 128 + 128)

                def body(k, carry):
                    rows = pl.ds(pl.multiple_of(k * 64, 64), 64)
                    renew(6, None, rows, cols, grads_ref[side, rows, :])
                    return carry

                lax.fori_loop(0, VOCAB // 64, body, 0)
                rest = grads_ref[side, tail_at : tail_at + OUTS - VOCAB, :].astype(F32)
                renew(6, None, slice(VOCAB, outs_all), cols, rest[0 : outs_all - VOCAB])
        else:
            count = here[15].shape[0]
            for side in range(2):
                cols = slice(side * 128, side * 128 + 128)
                grad = grads_ref[side, gains_at : gains_at + 16, :].astype(F32)[0:count]
                renew(5, None, slice(0, count), cols, grad)
        for move in moves(n, 1):
            move.start()
    for n in range(len(pieces)):
        for move in moves(n, 1):
            move.wait()


def update(grads, scal, state):
    layers = state[3].shape[0]
    anywhere = pl.BlockSpec(memory_space=pltpu.HBM)
    pieces = 4 * layers + 3
    return pl.pallas_call(
        functools.partial(update_kernel, layers),
        out_shape=tuple(jax.ShapeDtypeStruct(x.shape, F32) for x in state)
        + (jax.ShapeDtypeStruct((1, 1), F32),) * 3,
        in_specs=[
            pl.BlockSpec(memory_space=pltpu.SMEM),
            anywhere,
        ]
        + [anywhere] * 21,
        out_specs=(anywhere,) * 21 + (pl.BlockSpec(memory_space=pltpu.SMEM),) * 3,
        scratch_shapes=[pltpu.VMEM(x.shape, F32) for x in state]
        + [
            pltpu.SemaphoreType.DMA((pieces, 3)),
            pltpu.SemaphoreType.DMA((pieces, 3)),
            pltpu.SemaphoreType.DMA((pieces,)),
            pltpu.VMEM(grads.shape, BF),
        ],
        compiler_params=pltpu.CompilerParams(vmem_limit_bytes=62 * 1024 * 1024),
        name="update",
    )(scal, grads, *state)


def local(codes, actions, next_codes, lengths, rewards, continues, target_values, *state):
    state = state[0:18] + tuple(value.T for value in state[18:21])
    params = state[0::3]
    seq_size, dp_size = lax.axis_size("seq"), lax.axis_size("dp")
    sizes = (seq_size, dp_size)
    grads, scal = gradients(
        codes, actions, next_codes, lengths, rewards, continues, target_values, params, sizes
    )
    results = list(update(grads, scal, state))
    results[18:21] = [value.T for value in results[18:21]]
    results[21:24] = [value.reshape(()) for value in results[21:24]]
    return tuple(results)


def solution(mesh):
    rows, whole = P("dp", "seq"), P()
    return jax.shard_map(
        local,
        mesh=mesh,
        in_specs=(rows, rows, rows, P("dp", None), rows, rows, rows) + (whole,) * 21,
        out_specs=(whole,) * 24,
        check_vma=False,
    )
```

profile of v0, /device:TPU:0, one launch (start us, length us, event | category | flops | bytes accessed | tf_op | source)
XLA Modules:
  0.0 121.4 jit_solution(3188811116481453021)
XLA Ops:
  0.7 103.3 %train_step.1 = (bf16[2,7424,128]{2,1,0:T(8,128)(2,1)}, f32[8,128]{1,0:T(8,128)}) custom-call(s32[2,768]{1,0:T(2,128)} %codes_ref.1, s32[2,768]{1,0:T(2,128)} %actions_ref.1, s32[2,768]{1,0:T(2,128)} %next_ref.1, s32[2,8]{1,0:T(2,128)} %lengths_ref.1, f32[2,768]{1,0:T(2,128)} %rewards_ref.1, f32[2,768]{1,0:T(2,128)} %continues_ref.1, f32[2,768]{1,0:T(2,128)} %values_ref.1, ...), custom_call_target="tpu_custom_call" | custom-call | tf_op jit(solution)/shard_map/train_step/pallas_call | solution.py:1065
  104.0 17.2 %update.1 = (f32[530,256]{1,0:T(8,128)}, f32[530,256]{1,0:T(8,128)}, f32[530,256]{1,0:T(8,128)}, f32[2,256,768]{2,1,0:T(8,128)}, f32[2,256,768]{2,1,0:T(8,128)},...) custom-call(f32[8,128]{1,0:T(8,128)} %get-tuple-element.50.scal_ref,, ...), custom_call_target="tpu_custom_call" | custom-call | tf_op jit(solution)/shard_map/update/pallas_call | solution.py:1278
where the time goes:
time: 122 us; the launch traced here: 121 us
  Pallas kernels  121 us (99%)
    pallas_call x1, Pallas kernels, gradients(): pl.pallas_call(functools.partial(step_kernel, layers, sizes, buckets), ou...  103 us
    pallas_call x1, Pallas kernels, update(): pl.pallas_call(functools.partial(update_kernel, layers), out_shape=tuple(...  17.2 us

commit v1 on v0

--- a/solution.py
+++ b/solution.py
@@ -28,8 +28,9 @@
 BF = jnp.bfloat16
 F32 = jnp.float32
 ROWS = 256
-QRY = 2 * SEG
-KEY = 3 * SEG
+QRY = SEG
+KEY = QRY + SEG
+PER = 4
 OUTS = 544
 NEG = -1e30
 MESH = pl.DeviceIdType.MESH
@@ -359,7 +360,7 @@
         self.now += spent
         todo = []
         for n in sorted(self.due):
-            if self.due[n] + 0.3 <= self.now:
+            if self.due[n] + 0.8 <= self.now:
                 todo += self.plan_advance(n)
         return todo
 
@@ -640,15 +641,15 @@
         ids = iota((OUTS, ROWS), 0)
         return jnp.where((ids == code) | (ids == act), 1.0, 0.0).astype(BF)
 
-    def both_chunks(i):
-        return (2 * i, 2 * i + 1)
+    def three_chunks(i):
+        return tuple(3 * i + j for j in range(3))
 
     def embed(i, carry):
-        for c in both_chunks(i):
+        for c in three_chunks(i):
             xs[0, chunk_rows(c), :] += dot_tn(onehot(c), tb[...])
         return carry
 
-    lax.fori_loop(0, chunks // 2, embed, 0)
+    lax.fori_loop(0, chunks // 3, embed, 0)
 
     lane_head = iota((1, dims), 1) // head_dim
     group_mask = [jnp.where(lane_head // 2 == g, 1.0, 0.0).astype(BF) for g in range(groups)]
@@ -692,7 +693,7 @@
         gain = gains_ref[2 * layer : 2 * layer + 1, :]
 
         def body(i, carry):
-            pieces = [(c, chunk_rows(c)) for c in both_chunks(i)]
+            pieces = [(c, chunk_rows(c)) for c in three_chunks(i)]
             normed = [rms_apply(xs[2 * layer, rows, :], gain) for _, rows in pieces]
             wide = [dot_nn(h, wq[layer]).astype(BF) for h in normed]
             for (c, rows), h, qkv in zip(pieces, normed, wide):
@@ -701,7 +702,7 @@
                 kvs[layer, c // per_seq, kv_rows(c), :] = qkv[:, dims:]
             return carry
 
-        lax.fori_loop(0, chunks // 2, body, 0)
+        lax.fori_loop(0, chunks // 3, body, 0)
 
     def pair_rows(b, pair):
         return pl.ds(pl.multiple_of(b * span + pair * QRY, 16), QRY)
@@ -716,8 +717,8 @@
         copy = forward_copy(layer)
 
         def body(i, carry):
-            items = [(b, pairs - 1 - 2 * i - j) for j in range(2) for b in range(batch)]
-            pl.when(i == pairs // 2 - 1)(copy.wait)
+            items = [(b, pairs - 1 - PER * i - j) for j in range(PER) for b in range(batch)]
+            pl.when(i == pairs // PER - 1)(copy.wait)
             scores = []
             for b, pair in items:
                 keys = kvs[layer, b, pair_window(pair), 0:dims]
@@ -741,20 +742,20 @@
             return carry
 
         copy.start()
-        lax.fori_loop(0, pairs // 2, body, 0)
+        lax.fori_loop(0, pairs // PER, body, 0)
 
     def feed(layer):
         gain = gains_ref[2 * layer + 1 : 2 * layer + 2, :]
         c0, c1 = math.sqrt(2.0 / math.pi), 0.044715
 
         def body(i, carry):
-            pieces = [chunk_rows(c) for c in both_chunks(i)]
+            pieces = [chunk_rows(c) for c in three_chunks(i)]
             mids = [xs[2 * layer, rows, :] + dot_nn(mixes[layer, rows, :], wo[layer]) for rows in pieces]
             normed = [rms_apply(x, gain) for x in mids]
             for rows, x, h in zip(pieces, mids, normed):
                 xs[2 * layer + 1, rows, :] = x
                 hs[2 * layer + 1, rows, :] = h
-            hidden = [[], []]
+            hidden = [[], [], []]
             for j in range(ff // 256):
                 cols = slice(j * 256, j * 256 + 256)
                 for rows, h, parts in zip(pieces, normed, hidden):
@@ -771,7 +772,7 @@
                 xs[2 * layer + 2, rows, :] = x + dot_nn(act, wd[layer])
             return carry
 
-        lax.fori_loop(0, chunks // 2, body, 0)
+        lax.fori_loop(0, chunks // 3, body, 0)
 
     per_layer = 4 + 2 * (ff // 256)
     for layer in range(layers):
@@ -840,7 +841,7 @@
         return jnp.concatenate([grad_logits, (grad * valid).astype(BF)], axis=0)
 
     def losses(i, carry):
-        pieces = [(c, chunk_rows(c)) for c in both_chunks(i)]
+        pieces = [(c, chunk_rows(c)) for c in three_chunks(i)]
         hidden = [xs[2 * layers, rows, :] for _, rows in pieces]
         normed = [rms_apply(x, top_gain) for x in hidden]
         outs = [dot_nt(rt[...], h) for h in normed]
@@ -855,7 +856,7 @@
             dgain[2 * layers] += part
         return carry
 
-    lax.fori_loop(0, chunks // 2, losses, 0)
+    lax.fori_loop(0, chunks // 3, losses, 0)
     tail_at = VOCAB + layers * 12 * 256 + OUTS
     put(0, dot_nn(gouts[0:VOCAB, :], hs[2 * layers]))
     put(tail_at, dot_nn(gouts[VOCAB:OUTS, :], hs[2 * layers]))
@@ -881,8 +882,8 @@
         gain = gains_ref[2 * layer + 1 : 2 * layer + 2, :]
 
         def body(i):
-            pieces = [chunk_rows(c) for c in both_chunks(i)]
-            hidden = [[], []]
+            pieces = [chunk_rows(c) for c in three_chunks(i)]
+            hidden = [[], [], []]
             for j in range(ff // 256):
                 cols = slice(j * 256, j * 256 + 256)
                 for rows, parts in zip(pieces, hidden):
@@ -900,11 +901,11 @@
                 gl[rows, :] = low
                 dmix[rows, :] = dot_nt(low, wo[layer]).astype(BF)
 
-        spread(chunks // 2, 3.3, body)
+        spread(chunks // 3, 3.3, body)
 
     def attend_back(layer):
         def steps(i):
-            items = [(b, 2 * i + j) for j in range(2) for b in range(batch)]
+            items = [(b, PER * i + j) for j in range(PER) for b in range(batch)]
             keys, values, queries, douts = [], [], [], []
             for b, pair in items:
                 window, rows = pair_window(pair), pair_rows(b, pair)
@@ -937,10 +938,11 @@
             before = [carried[b] + wide[b][0:SEG] for b in range(batch)]
             for at, (b, pair) in enumerate(items):
                 rows = pl.multiple_of(b * span + pair * QRY, 16)
-                dqkv[pl.ds(rows, SEG), dims:] = wide[at][SEG:QRY].astype(BF)
+                if QRY > SEG:
+                    dqkv[pl.ds(rows, QRY - SEG), dims:] = wide[at][SEG:QRY].astype(BF)
                 if at + batch < len(items):
                     ending = wide[at][QRY:] + wide[at + batch][0:SEG]
-                    dqkv[pl.ds(pl.multiple_of(rows + SEG, 16), SEG), dims:] = ending.astype(BF)
+                    dqkv[pl.ds(pl.multiple_of(rows + QRY - SEG, 16), SEG), dims:] = ending.astype(BF)
                 else:
                     carried[b] = wide[at][QRY:]
             return before
@@ -959,11 +961,11 @@
             @pl.when(i > 0)
             def _():
                 for b in range(batch):
-                    rows = pl.ds(pl.multiple_of(b * span + i * 2 * QRY - SEG, 16), SEG)
+                    rows = pl.ds(pl.multiple_of(b * span + i * PER * QRY - SEG, 16), SEG)
                     dqkv[rows, dims:] = before[b]
 
         carried[...] = jnp.zeros_like(carried)
-        spread(pairs // 2, 6.8, body)
+        spread(pairs // PER, 6.0, body)
         copy.wait()
         for b in range(batch):
             final = carried[b] + brecv[layer, b].astype(F32)
@@ -973,7 +975,7 @@
         gain = gains_ref[2 * layer : 2 * layer + 1, :]
 
         def body(i):
-            pieces = [chunk_rows(c) for c in both_chunks(i)]
+            pieces = [chunk_rows(c) for c in three_chunks(i)]
             pulled = [dot_nt(dqkv[rows, :], wq[layer]) for rows in pieces]
             for rows, dh in zip(pieces, pulled):
                 grad_x, part = rms_pull(dh, xs[2 * layer, rows, :], gain)
@@ -982,7 +984,7 @@
                 gx[rows, :] = grad
                 gl[rows, :] = grad.astype(BF)
 
-        spread(chunks // 2, 1.5, body)
+        spread(chunks // 3, 1.5, body)
 
     at = VOCAB
     bucket = 0

time: 122 us -> 117 us (0.959)
  Pallas kernels: 121 us -> 116 us
    pallas_call x1, Pallas kernels: 103 us -> 98.7 us  [gradients(): pl.pallas_call(functools.partial(step_kernel, layers, sizes, buckets), ou...]
where the time goes in v1:
time: 117 us
  Pallas kernels  116 us (99%)
    pallas_call x1, Pallas kernels, gradients(): pl.pallas_call(functools.partial(step_kernel, layers, sizes, buckets), ou...  98.7 us
    pallas_call x1, Pallas kernels, update(): pl.pallas_call(functools.partial(update_kernel, layers), out_shape=tuple(...  17.2 us

profile of v1, /device:TPU:0, one launch (start us, length us, event | category | flops | bytes accessed | tf_op | source)
XLA Modules:
  0.0 116.8 jit_solution(973352238332817818)
XLA Ops:
  0.7 98.7 %train_step.1 = (bf16[2,7424,128]{2,1,0:T(8,128)(2,1)}, f32[8,128]{1,0:T(8,128)}) custom-call(s32[2,768]{1,0:T(2,128)} %codes_ref.1, s32[2,768]{1,0:T(2,128)} %actions_ref.1, s32[2,768]{1,0:T(2,128)} %next_ref.1, s32[2,8]{1,0:T(2,128)} %lengths_ref.1, f32[2,768]{1,0:T(2,128)} %rewards_ref.1, f32[2,768]{1,0:T(2,128)} %continues_ref.1, f32[2,768]{1,0:T(2,128)} %values_ref.1, ...), custom_call_target="tpu_custom_call" | custom-call | tf_op jit(solution)/shard_map/train_step/pallas_call | solution.py:1067
  99.4 17.2 %update.1 = (f32[530,256]{1,0:T(8,128)}, f32[530,256]{1,0:T(8,128)}, f32[530,256]{1,0:T(8,128)}, f32[2,256,768]{2,1,0:T(8,128)}, f32[2,256,768]{2,1,0:T(8,128)},...) custom-call(f32[8,128]{1,0:T(8,128)} %get-tuple-element.50.scal_ref,, ...), custom_call_target="tpu_custom_call" | custom-call | tf_op jit(solution)/shard_map/update/pallas_call | solution.py:1280

commit v2 on v1

--- a/solution.py
+++ b/solution.py
@@ -611,7 +611,7 @@
             xs[0, rows, half:dims] = here_cos * start_cos + here_sin * start_sin
         return carry
 
-    lax.fori_loop(0, tiles, marks, 0)
+    lax.fori_loop(0, tiles, marks, 0, unroll=4)
 
     def lowest(pair, carry):
         within = lax.rem(iota((8, groups * QRY), 1), QRY)
@@ -624,7 +624,7 @@
             lows[b * pairs + pair] = jnp.maximum(low, -first)
         return carry
 
-    lax.fori_loop(0, pairs, lowest, 0)
+    lax.fori_loop(0, pairs, lowest, 0, unroll=4)
 
     def chunk_rows(c):
         return pl.ds(pl.multiple_of(c * ROWS, ROWS), ROWS)
@@ -645,11 +645,11 @@
         return tuple(3 * i + j for j in range(3))
 
     def embed(i, carry):
-        for c in three_chunks(i):
+        for c in range(chunks):
             xs[0, chunk_rows(c), :] += dot_tn(onehot(c), tb[...])
         return carry
 
-    lax.fori_loop(0, chunks // 3, embed, 0)
+    lax.fori_loop(0, 1, embed, 0)
 
     lane_head = iota((1, dims), 1) // head_dim
     group_mask = [jnp.where(lane_head // 2 == g, 1.0, 0.0).astype(BF) for g in range(groups)]
@@ -693,7 +693,7 @@
         gain = gains_ref[2 * layer : 2 * layer + 1, :]
 
         def body(i, carry):
-            pieces = [(c, chunk_rows(c)) for c in three_chunks(i)]
+            pieces = [(c, chunk_rows(c)) for c in range(chunks)]
             normed = [rms_apply(xs[2 * layer, rows, :], gain) for _, rows in pieces]
             wide = [dot_nn(h, wq[layer]).astype(BF) for h in normed]
             for (c, rows), h, qkv in zip(pieces, normed, wide):
@@ -702,7 +702,7 @@
                 kvs[layer, c // per_seq, kv_rows(c), :] = qkv[:, dims:]
             return carry
 
-        lax.fori_loop(0, chunks // 3, body, 0)
+        lax.fori_loop(0, 1, body, 0)
 
     def pair_rows(b, pair):
         return pl.ds(pl.multiple_of(b * span + pair * QRY, 16), QRY)

time: 117 us -> 116 us (level)
  no operation moved by 1% of the time
where the time goes in v2:
time: 116 us
  Pallas kernels  115 us (99%)
    pallas_call x1, Pallas kernels, gradients(): pl.pallas_call(functools.partial(step_kernel, layers, sizes, buckets), ou...  97.6 us
    pallas_call x1, Pallas kernels, update(): pl.pallas_call(functools.partial(update_kernel, layers), out_shape=tuple(...  17.2 us

profile of v2, /device:TPU:0, one launch (start us, length us, event | category | flops | bytes accessed | tf_op | source)
XLA Modules:
  0.0 115.6 jit_solution(17194578364244897296)
XLA Ops:
  0.7 97.6 %train_step.1 = (bf16[2,7424,128]{2,1,0:T(8,128)(2,1)}, f32[8,128]{1,0:T(8,128)}) custom-call(s32[2,768]{1,0:T(2,128)} %codes_ref.1, s32[2,768]{1,0:T(2,128)} %actions_ref.1, s32[2,768]{1,0:T(2,128)} %next_ref.1, s32[2,8]{1,0:T(2,128)} %lengths_ref.1, f32[2,768]{1,0:T(2,128)} %rewards_ref.1, f32[2,768]{1,0:T(2,128)} %continues_ref.1, f32[2,768]{1,0:T(2,128)} %values_ref.1, ...), custom_call_target="tpu_custom_call" | custom-call | tf_op jit(solution)/shard_map/train_step/pallas_call | solution.py:1067
  98.2 17.2 %update.1 = (f32[530,256]{1,0:T(8,128)}, f32[530,256]{1,0:T(8,128)}, f32[530,256]{1,0:T(8,128)}, f32[2,256,768]{2,1,0:T(8,128)}, f32[2,256,768]{2,1,0:T(8,128)},...) custom-call(f32[8,128]{1,0:T(8,128)} %get-tuple-element.50.scal_ref,, ...), custom_call_target="tpu_custom_call" | custom-call | tf_op jit(solution)/shard_map/update/pallas_call | solution.py:1280
